TPU v7x, 128 devices: a whole 4x4x4 slice. The times are simulated.
128 devices in a mesh: frame: 8 (over x, core), cell: 16 (over y, z).
Axes of the slice: x: 4, y: 4, z: 4, core: 2. Of those that a mesh axis runs over, the one named last changes fastest.
Arguments:
- front: float32 [8, 4096, 4096], P('frame', 'cell')
- parent_of: int32 [8], replicated, may hold values from 0 to 7
- block_map: int32 [8, 13], replicated, may hold values from 3 to 31, as said below
- parent_in: bfloat16 [8, 2, 4096, 8192], P('frame', None, 'cell'), may hold values from -0.3125 to 0.3125
Outputs:
- lower_panel: float32 [8, 4096, 768], P('frame', 'cell')
- parent_out: bfloat16 [8, 2, 4096, 8192], P('frame', None, 'cell')
Inputs may be any that keep to these rules, and one draw needn't show every extreme that they name: block_map[c, k] is 3 + k or 3 + k + 16.
All inputs are finite; a program needn't handle non-finite values.
Results may differ from a plain program's by a relative error of at most 0.004.
Values may be sent and summed in bfloat16 or wider, within the bound.
A program may use at most 192 MiB of HBM per device.

v0:
```python
import jax
import jax.numpy as jnp
from jax import lax
from jax.sharding import PartitionSpec as P

PB = 3


def per_device(front, parent_of, block_map, parent_in):
    block_row = front[0]
    rows_here = block_row.shape[0]
    order = block_row.shape[1]
    blocks = order // rows_here
    width = PB * rows_here
    cell_index = lax.axis_index("cell")
    frame_index = lax.axis_index("frame")
    highest = lax.Precision.HIGHEST
    panel = lax.all_gather(block_row[:, :width], "cell", axis=0, tiled=True)
    l11 = jnp.linalg.cholesky(panel[:width])
    l21 = lax.linalg.triangular_solve(
        l11, panel[width:], left_side=False, lower=True, transpose_a=True
    )
    lower_all = jnp.concatenate([l11, l21], 0)
    my_lower = lax.dynamic_slice_in_dim(lower_all, cell_index * rows_here, rows_here, 0)
    product = jnp.dot(my_lower, l21.T, precision=highest)
    update = (block_row[:, width:] - product).astype(jnp.bfloat16)
    update_blocks = update.shape[1] // rows_here
    which_k = jnp.maximum(cell_index - PB, 0)
    whole_parent = parent_in[0].reshape(2, rows_here, 2, blocks, rows_here)
    region_start = whole_parent[:, :, :, PB:, :].astype(jnp.float32)
    pieces = lax.all_gather(update[None], "frame", axis=0, tiled=True)

    def one_child(step, acc):
        parent = lax.dynamic_index_in_dim(parent_of, step, 0, keepdims=False)
        positions = lax.dynamic_index_in_dim(block_map, step, 0, keepdims=False)
        target = lax.dynamic_index_in_dim(positions, which_k, 0, keepdims=False)
        live = (parent == frame_index) & (cell_index >= PB)
        half = target // blocks

        def add_piece(inner):
            piece = lax.dynamic_index_in_dim(pieces, step, 0, keepdims=False)
            piece = piece.reshape(rows_here, update_blocks, rows_here).astype(jnp.float32)
            upper = (positions >= blocks)[None, :, None]
            zeros = jnp.zeros_like(piece)
            delta = jnp.stack([jnp.where(upper, zeros, piece), jnp.where(upper, piece, zeros)], 1)
            current = lax.dynamic_index_in_dim(inner, half, 0, keepdims=False)
            return lax.dynamic_update_index_in_dim(inner, current + delta, half, 0)

        def keep_same(inner):
            return inner

        return lax.cond(live, add_piece, keep_same, acc)

    total = lax.fori_loop(0, pieces.shape[0], one_child, region_start)
    merged = jnp.concatenate([whole_parent[:, :, :, :PB, :], total.astype(jnp.bfloat16)], 3)
    merged = merged.reshape(2, rows_here, 2 * blocks * rows_here)
    return (my_lower[None], merged[None])


def solution(mesh):
    placed = (P("frame", "cell", None), P(), P(), P("frame", None, "cell", None))
    return jax.shard_map(
        per_device,
        mesh=mesh,
        in_specs=placed,
        out_specs=(P("frame", "cell", None), P("frame", None, "cell", None)),
        check_vma=False,
    )
```

profile of v0, /device:TPU:15, one launch (start us, length us, event | category | flops | bytes accessed | tf_op | source)
XLA Modules:
  0.0 594.5 jit_solution(12432647070224209038)
XLA Ops:
  15.0 101.0 %all-gather.4.cloned.1.call-done = f32[4096,768]{0,1:T(8,128)} async-done(((f32[256,768]{0,1:T(8,128)}), f32[4096,768]{0,1:T(8,128)}) %all-gather.4.cloned.1.call-update) | async-done | bytes 12582928 | tf_op jit(solution)/shard_map/all_gather | solution.py:18
  123.7 11.7 %cholesky.165 = f32[128,128]{1,0:T(8,128)S(1)} custom-call(f32[128,128]{1,0:T(8,128)S(1)} %cholesky.424), custom_call_target="Cholesky" | custom-call | tf_op jit(solution)/shard_map/jit(cholesky)/cholesky | solution.py:19
  135.4 9.8 %custom-call.46 = f32[1,128,128]{1,2,0:T(8,128)S(1)} custom-call(f32[1,128,128]{2,1,0:T(8,128)S(1)} %get-tuple-element.497), custom_call_target="InvertDiagBlocksLowerTriangular" | custom-call | tf_op jit(solution)/shard_map/jit(cholesky)/cholesky | solution.py:19
  148.2 11.7 %cholesky.188 = f32[128,128]{1,0:T(8,128)S(1)} custom-call(f32[128,128]{1,0:T(8,128)S(1)} %cholesky.428), custom_call_target="Cholesky" | custom-call | tf_op jit(solution)/shard_map/jit(cholesky)/cholesky | solution.py:19
  160.0 10.1 %custom-call.47 = f32[1,128,128]{1,2,0:T(8,128)S(1)} custom-call(f32[1,128,128]{2,1,0:T(8,128)S(1)} %get-tuple-element.494), custom_call_target="InvertDiagBlocksLowerTriangular" | custom-call | tf_op jit(solution)/shard_map/jit(cholesky)/cholesky | solution.py:19
  172.0 11.7 %cholesky.354 = f32[128,128]{1,0:T(8,128)S(1)} custom-call(f32[128,128]{1,0:T(8,128)S(1)} %cholesky.433), custom_call_target="Cholesky" | custom-call | tf_op jit(solution)/shard_map/jit(cholesky)/cholesky | solution.py:19
  184.4 9.8 %custom-call.48 = f32[1,128,128]{1,2,0:T(8,128)S(1)} custom-call(f32[1,128,128]{2,1,0:T(8,128)S(1)} %get-tuple-element.491), custom_call_target="InvertDiagBlocksLowerTriangular" | custom-call | tf_op jit(solution)/shard_map/jit(cholesky)/cholesky | solution.py:19
  196.1 11.9 %cholesky.373 = f32[128,128]{1,0:T(8,128)S(1)} custom-call(f32[128,128]{1,0:T(8,128)S(1)} %cholesky.438), custom_call_target="Cholesky" | custom-call | tf_op jit(solution)/shard_map/jit(cholesky)/cholesky | solution.py:19
  208.7 9.8 %custom-call.49 = f32[1,128,128]{1,2,0:T(8,128)S(1)} custom-call(f32[1,128,128]{2,1,0:T(8,128)S(1)} %get-tuple-element.488), custom_call_target="InvertDiagBlocksLowerTriangular" | custom-call | tf_op jit(solution)/shard_map/jit(cholesky)/cholesky | solution.py:19
  220.3 11.7 %cholesky.392 = f32[128,128]{1,0:T(8,128)S(1)} custom-call(f32[128,128]{1,0:T(8,128)S(1)} %cholesky.443), custom_call_target="Cholesky" | custom-call | tf_op jit(solution)/shard_map/jit(cholesky)/cholesky | solution.py:19
  232.7 9.8 %custom-call.50 = f32[1,128,128]{1,2,0:T(8,128)S(1)} custom-call(f32[1,128,128]{2,1,0:T(8,128)S(1)} %get-tuple-element.485), custom_call_target="InvertDiagBlocksLowerTriangular" | custom-call | tf_op jit(solution)/shard_map/jit(cholesky)/cholesky | solution.py:19
  244.0 12.1 %cholesky.410 = f32[128,128]{1,0:T(8,128)S(1)} custom-call(f32[128,128]{1,0:T(8,128)S(1)} %convolution_subtract_fusion.8), custom_call_target="Cholesky" | custom-call | tf_op jit(solution)/shard_map/jit(cholesky)/cholesky | solution.py:19
  263.5 17.4 %while.21 = (s32[]{:T(128)}, f32[768,768]{1,0:T(8,128)}, s32[6,2]{0,1:T(2,128)S(1)}, f32[6,128,128]{2,1,0:T(8,128)S(1)}, s32[]{:T(128)}) while((s32[]{:T(128)}, f32[768,768]{1,0:T(8,128)}, s32[6,2]{0,1:T(2,128)S(1)}, f32[6,128,128]{2,1,0:T(8,128)S(1)}, s32[]{:T(128)}) %tuple.115), condition=%wide.while_cond, body=%wide.while_body.sunk | while | flops 2 | bytes 131181 | solution.py:20
  281.0 59.0 %custom-call.51 = f32[6,128,128]{1,2,0:T(8,128)S(1)} custom-call(f32[6,128,128]{2,1,0:T(8,128)S(1)} %get-tuple-element.425), custom_call_target="InvertDiagBlocksLowerTriangular" | custom-call | tf_op jit(solution)/shard_map/triangular_solve | solution.py:20
  393.8 18.2 %fusion.9 = bf16[256,3328]{0,1:T(8,128)(2,1)} fusion(f32[256,768]{0,1:T(8,128)S(1)} %fusion.29, f32[3328,768]{0,1:T(8,128)S(1)} %convolution_dynamic-update-slice_fusion, f32[256,4096]{0,1:T(8,128)S(1)} %bitcast.109), kind=kOutput, calls=%fused_computation.24 | convolution fusion | flops 7853441024 | bytes 16121856 | tf_op jit(solution)/shard_map/dot_general | solution.py:25
  412.0 12.0 %copy.15 = bf16[1,2,256,8192]{2,3,1,0:T(8,128)(2,1)} copy(bf16[1,2,256,8192]{3,2,1,0:T(8,128)(2,1)} %param.11) | data formatting | bytes 16777216 | tf_op args[3]
  425.7 9.8 %slice_convert_fusion = f32[2,256,2,13,256]{1,4,3,2,0:T(8,128)} fusion(bf16[2,256,2,16,256]{1,4,3,2,0:T(8,128)(2,1)} %bitcast.103), kind=kLoop, calls=%fused_computation.13 | loop fusion | flops 3407872 | bytes 20447232 | tf_op jit(solution)/shard_map/convert_element_type | solution.py:30
  436.7 52.1 %all-gather.6.cloned.1.call-done = bf16[2048,3328]{0,1:T(8,128)(2,1)} async-done(((bf16[256,3328]{0,1:T(8,128)(2,1)}), bf16[2048,3328]{0,1:T(8,128)(2,1)}) %all-gather.6.cloned.1.call-update) | async-done | bytes 13631504 | tf_op jit(solution)/shard_map/all_gather | solution.py:31
  488.8 12.5 %copy.23 = bf16[416,8,8,256]{3,2,0,1:T(8,128)(2,1)} copy(bf16[416,8,8,256]{3,2,1,0:T(8,128)(2,1)} %bitcast.112) | data formatting | bytes 27262976 | tf_op jit(solution)/shard_map/all_gather | solution.py:31
  501.3 58.4 %while.20 = (s32[]{:T(128)}, f32[2,256,2,13,256]{1,4,3,2,0:T(8,128)}, s32[8]{0:T(128)S(1)}, s32[]{:T(128)}, pred[]{:T(512)}, /*index=5*/s32[8,13]{1,0:T(8,128)},...) while((s32[]{:T(128)}, f32[2,256,2,13,256]{1,4,3,2,0:T(8,128)}, ...), condition=%wide.region_15.16_spmd, body=%wide.region_12.15_spmd.sunk | while | flops 5963816 | bytes 32375320 | solution.py:54
  504.1 12.4 %conditional.2 = (f32[2,256,2,13,256]{1,4,3,2,0:T(8,128)}) conditional(s32[]{:T(128)} %convert_element_type.50, f32[2,256,2,13,256]{1,4,3,2,0:T(8,128)} %get-tuple-element.611, (s32[]{:T(128)}, s32[]{:T(128)}, f32[2,256,2,13,256]{1,4,3,2,0:T(8,128)}, s32[8,13]{1,0:T(8,128)}, s32[]{:T(128)}, /*index=5*/bf16[8,256,3328]{1,2,0:T(8,128)(2,1)}, ...), branch_computations={%region_13.13_spmd, %region_14.14_spmd} | conditional | flops 5963810 | bytes 32375100 | solution.py:52
  527.0 12.5 %conditional.2 = (f32[2,256,2,13,256]{1,4,3,2,0:T(8,128)}) conditional(s32[]{:T(128)} %convert_element_type.50, f32[2,256,2,13,256]{1,4,3,2,0:T(8,128)} %get-tuple-element.611, (s32[]{:T(128)}, s32[]{:T(128)}, f32[2,256,2,13,256]{1,4,3,2,0:T(8,128)}, s32[8,13]{1,0:T(8,128)}, s32[]{:T(128)}, /*index=5*/bf16[8,256,3328]{1,2,0:T(8,128)(2,1)}, ...), branch_computations={%region_13.13_spmd, %region_14.14_spmd} | conditional | flops 5963810 | bytes 32375100 | solution.py:52
  542.0 12.4 %conditional.2 = (f32[2,256,2,13,256]{1,4,3,2,0:T(8,128)}) conditional(s32[]{:T(128)} %convert_element_type.50, f32[2,256,2,13,256]{1,4,3,2,0:T(8,128)} %get-tuple-element.611, (s32[]{:T(128)}, s32[]{:T(128)}, f32[2,256,2,13,256]{1,4,3,2,0:T(8,128)}, s32[8,13]{1,0:T(8,128)}, s32[]{:T(128)}, /*index=5*/bf16[8,256,3328]{1,2,0:T(8,128)(2,1)}, ...), branch_computations={%region_13.13_spmd, %region_14.14_spmd} | conditional | flops 5963810 | bytes 32375100 | solution.py:52
  575.2 12.0 %copy.20 = bf16[1,2,256,8192]{3,2,1,0:T(8,128)(2,1)} copy(bf16[1,2,256,8192]{2,3,1,0:T(8,128)(2,1)} %bitcast.104) | data formatting | bytes 16777216 | tf_op jit(solution)/shard_map/broadcast_in_dim;reshape | solution.py:57
  (128 shorter events, 165.5 us)
Async XLA Ops:
  7.2 108.8 %all-gather.4.cloned.1.call-start = ((), (), s32[]{:S(2)}) async-start(), calls=%async_computation | async-start | bytes 13369344 | tf_op jit(solution)/shard_map/all_gather | solution.py:18
  14.9 473.9 %all-gather.6.cloned.1.call-start = ((), (), s32[]{:S(2)}) async-start(), calls=%async_computation.1 | async-start | bytes 15335424 | tf_op jit(solution)/shard_map/all_gather | solution.py:31
  115.9 1.7 slice-start.3
  122.3 1.4 copy-start.3
  339.9 8.6 %copy-start.4 = (f32[6,128,128]{1,2,0:T(8,128)}, f32[6,128,128]{1,2,0:T(8,128)S(1)}, u32[]{:S(2)}) copy-start(f32[6,128,128]{1,2,0:T(8,128)S(1)} %custom-call.51) | copy-start | bytes 1179652
  345.2 14.6 %slice-start = ((s8[12582912]{0:T(1024)(128)(4,1)}), s8[4194304]{0:T(1024)(128)(4,1)S(1)}, s32[]{:S(2)}) async-start(s8[12582912]{0:T(1024)(128)(4,1)} %bitcast.110), calls=%async_computation.2 | async-start | bytes 8388608
  348.5 11.3 %slice-start.1 = ((s8[12582912]{0:T(1024)(128)(4,1)}), s8[4194304]{0:T(1024)(128)(4,1)S(1)}, s32[]{:S(2)}) async-start(s8[12582912]{0:T(1024)(128)(4,1)} %bitcast.110), calls=%async_computation.3 | async-start | bytes 8388608
  350.3 9.6 %slice-start.2 = ((s8[12582912]{0:T(1024)(128)(4,1)}), s8[4194304]{0:T(1024)(128)(4,1)S(1)}, s32[]{:S(2)}) async-start(s8[12582912]{0:T(1024)(128)(4,1)} %bitcast.110), calls=%async_computation.4 | async-start | bytes 8388608
  356.6 3.2 copy-start.1
  359.9 5.0 copy-start.2
  391.6 2.2 copy-start
  488.8 12.5 %copy-start.5 = (s32[8]{0:T(128)S(1)}, s32[8]{0:T(128)}, u32[]{:S(2)}) copy-start(s32[8]{0:T(128)} %param.9) | copy-start | bytes 100
Sparse Core Ops, SparseCore 0:
  15.0 100.8 all-gather.3
  412.1 76.6 all-gather.5
where the time goes:
time: 606 us; the launch traced here: 594 us
  other arithmetic  238 us (39%)
  waiting for transfers between devices  153 us (25%)
  local copies, waits for them, and re-layouts  97.1 us (16%)
  matrix products  74 us (12%)
  between operations  18.5 us (3%)
  loops' own time  14 us (2%)
    another operation x22, other arithmetic, per_device(): l11 = jnp.linalg.cholesky(panel[:width])  124 us
    all_gather x1, waiting for transfers between devices, per_device(): panel = lax.all_gather(block_row[:, :width], 'cell', axis=0, tiled=True)  101 us
    another operation x3, other arithmetic, per_device(): lax.linalg.triangular_solve(l11, panel[width:], left_side=False, lower=Tr...  61.4 us
    all_gather x1, waiting for transfers between devices, per_device(): pieces = lax.all_gather(update[None], 'frame', axis=0, tiled=True)  52.1 us
    another operation x11, matrix products, per_device(): lax.linalg.triangular_solve(l11, panel[width:], left_side=False, lower=Tr...  46.1 us
    unnamed x20, local copies, waits for them, and re-layouts  24.3 us
    dynamic_update_slice x3, other arithmetic, add_piece(): return lax.dynamic_update_index_in_dim(inner, current + delta, half, 0)  19.8 us
    dot_general x1, matrix products, per_device(): product = jnp.dot(my_lower, l21.T, precision=highest)  18.2 us
  transfers between devices with their start and end apart: 2, of which 2 were waited for; matrix products, arithmetic and copies ran while one was open for 4% of the time, Pallas kernels for 0%

commit v1 on v0

--- a/solution.py
+++ b/solution.py
@@ -2,8 +2,20 @@
 import jax.numpy as jnp
 from jax import lax
 from jax.sharding import PartitionSpec as P
+from jax.lax import axis_index, ppermute, psum
 
 PB = 3
+
+
+def wait_flows_up(inputs, on_dim=0):
+    ndev = psum(1, "frame")
+    heap = [inputs]
+    for j in range(ndev - 1):
+        block_now = ppermute(heap[-1], "frame", [(j0, (j0 + 1) % ndev) for j0 in range(ndev)])
+        heap.append(block_now)
+    later = jnp.concatenate(heap[::-1], on_dim)
+    row_out = axis_index("frame")
+    return jnp.roll(later, (row_out + 1) * inputs.shape[on_dim], on_dim)
 
 
 def per_device(front, parent_of, block_map, parent_in):
@@ -28,7 +40,7 @@
     which_k = jnp.maximum(cell_index - PB, 0)
     whole_parent = parent_in[0].reshape(2, rows_here, 2, blocks, rows_here)
     region_start = whole_parent[:, :, :, PB:, :].astype(jnp.float32)
-    pieces = lax.all_gather(update[None], "frame", axis=0, tiled=True)
+    pieces = wait_flows_up(update[None])
 
     def one_child(step, acc):
         parent = lax.dynamic_index_in_dim(parent_of, step, 0, keepdims=False)

time: 606 us -> 702 us (1.16)
  waiting for transfers between devices: 153 us -> 214 us
  starting transfers between devices: 0.08 us -> 24 us
  local copies, waits for them, and re-layouts: 97.1 us -> 110 us
    ppermute x0 -> x7, waiting for transfers between devices: none -> 113 us  [wait_flows_up(): ppermute(heap[-1], 'frame', [(j0, (j0 + 1) % ndev) for j0 in range(ndev)])]
    all_gather x1 -> x0, waiting for transfers between devices: 52.1 us -> none  [per_device(): pieces = lax.all_gather(update[None], 'frame', axis=0, tiled=True)]
    ppermute x0 -> x7, starting transfers between devices: none -> 24 us  [wait_flows_up(): ppermute(heap[-1], 'frame', [(j0, (j0 + 1) % ndev) for j0 in range(ndev)])]
    unnamed x20 -> x61, local copies, waits for them, and re-layouts: 24.3 us -> 43.5 us
    all_gather x1 -> x0, local copies, waits for them, and re-layouts: 12.5 us -> none  [per_device(): pieces = lax.all_gather(update[None], 'frame', axis=0, tiled=True)]
  transfers between devices with their start and end apart: 2 -> 8, of which waited for: 2 -> 7; matrix products, arithmetic and copies ran while one was open for 4% -> 4% of each run, Pallas kernels for 0% -> 0%
where the time goes in v1:
time: 702 us; the launch traced here: 690 us
  other arithmetic  238 us (34%)
  waiting for transfers between devices  214 us (30%)
  local copies, waits for them, and re-layouts  110 us (16%)
  matrix products  73.6 us (10%)
  starting transfers between devices  24 us (3%)
  between operations  18.7 us (3%)
  loops' own time  12.3 us (2%)
    another operation x22, other arithmetic, per_device(): l11 = jnp.linalg.cholesky(panel[:width])  124 us
    ppermute x7, waiting for transfers between devices, wait_flows_up(): ppermute(heap[-1], 'frame', [(j0, (j0 + 1) % ndev) for j0 in range(ndev)])  113 us
    all_gather x1, waiting for transfers between devices, per_device(): panel = lax.all_gather(block_row[:, :width], 'cell', axis=0, tiled=True)  101 us
    another operation x3, other arithmetic, per_device(): lax.linalg.triangular_solve(l11, panel[width:], left_side=False, lower=Tr...  61.4 us
    another operation x11, matrix products, per_device(): lax.linalg.triangular_solve(l11, panel[width:], left_side=False, lower=Tr...  46.3 us
    unnamed x61, local copies, waits for them, and re-layouts  43.5 us
    ppermute x7, starting transfers between devices, wait_flows_up(): ppermute(heap[-1], 'frame', [(j0, (j0 + 1) % ndev) for j0 in range(ndev)])  24 us
    dynamic_update_slice x3, other arithmetic, add_piece(): return lax.dynamic_update_index_in_dim(inner, current + delta, half, 0)  19.8 us
  transfers between devices with their start and end apart: 8, of which 7 were waited for; matrix products, arithmetic and copies ran while one was open for 4% of the time, Pallas kernels for 0%

profile of v1, /device:TPU:15, one launch (start us, length us, event | category | flops | bytes accessed | tf_op | source)
XLA Modules:
  0.0 690.3 jit_solution(11636617548586124716)
XLA Ops:
  14.9 101.0 %all-gather.2.cloned.1.call-done = f32[4096,768]{0,1:T(8,128)} async-done(((f32[256,768]{0,1:T(8,128)}), f32[4096,768]{0,1:T(8,128)}) %all-gather.2.cloned.1.call-update) | async-done | bytes 12582928 | tf_op jit(solution)/shard_map/all_gather | solution.py:30
  123.6 11.7 %cholesky.165 = f32[128,128]{1,0:T(8,128)S(1)} custom-call(f32[128,128]{1,0:T(8,128)S(1)} %cholesky.424), custom_call_target="Cholesky" | custom-call | tf_op jit(solution)/shard_map/jit(cholesky)/cholesky | solution.py:31
  135.4 9.8 %custom-call.46 = f32[1,128,128]{1,2,0:T(8,128)S(1)} custom-call(f32[1,128,128]{2,1,0:T(8,128)S(1)} %get-tuple-element.489), custom_call_target="InvertDiagBlocksLowerTriangular" | custom-call | tf_op jit(solution)/shard_map/jit(cholesky)/cholesky | solution.py:31
  148.2 11.7 %cholesky.188 = f32[128,128]{1,0:T(8,128)S(1)} custom-call(f32[128,128]{1,0:T(8,128)S(1)} %cholesky.428), custom_call_target="Cholesky" | custom-call | tf_op jit(solution)/shard_map/jit(cholesky)/cholesky | solution.py:31
  159.9 9.9 %custom-call.47 = f32[1,128,128]{1,2,0:T(8,128)S(1)} custom-call(f32[1,128,128]{2,1,0:T(8,128)S(1)} %get-tuple-element.486), custom_call_target="InvertDiagBlocksLowerTriangular" | custom-call | tf_op jit(solution)/shard_map/jit(cholesky)/cholesky | solution.py:31
  171.8 11.7 %cholesky.354 = f32[128,128]{1,0:T(8,128)S(1)} custom-call(f32[128,128]{1,0:T(8,128)S(1)} %cholesky.433), custom_call_target="Cholesky" | custom-call | tf_op jit(solution)/shard_map/jit(cholesky)/cholesky | solution.py:31
  196.0 12.1 %cholesky.373 = f32[128,128]{1,0:T(8,128)S(1)} custom-call(f32[128,128]{1,0:T(8,128)S(1)} %cholesky.438), custom_call_target="Cholesky" | custom-call | tf_op jit(solution)/shard_map/jit(cholesky)/cholesky | solution.py:31
  220.3 11.7 %cholesky.392 = f32[128,128]{1,0:T(8,128)S(1)} custom-call(f32[128,128]{1,0:T(8,128)S(1)} %cholesky.443), custom_call_target="Cholesky" | custom-call | tf_op jit(solution)/shard_map/jit(cholesky)/cholesky | solution.py:31
  244.1 11.9 %cholesky.410 = f32[128,128]{1,0:T(8,128)S(1)} custom-call(f32[128,128]{1,0:T(8,128)S(1)} %convolution_subtract_fusion.8), custom_call_target="Cholesky" | custom-call | tf_op jit(solution)/shard_map/jit(cholesky)/cholesky | solution.py:31
  263.5 18.1 %while.21 = (s32[]{:T(128)}, f32[768,768]{1,0:T(8,128)}, s32[6,2]{0,1:T(2,128)S(1)}, f32[6,128,128]{2,1,0:T(8,128)S(1)}, s32[]{:T(128)}) while((s32[]{:T(128)}, f32[768,768]{1,0:T(8,128)}, s32[6,2]{0,1:T(2,128)S(1)}, f32[6,128,128]{2,1,0:T(8,128)S(1)}, s32[]{:T(128)}) %tuple.114), condition=%wide.while_cond, body=%wide.while_body.sunk | while | flops 2 | bytes 131181 | solution.py:32
  281.7 59.0 %custom-call.51 = f32[6,128,128]{1,2,0:T(8,128)S(1)} custom-call(f32[6,128,128]{2,1,0:T(8,128)S(1)} %get-tuple-element.425), custom_call_target="InvertDiagBlocksLowerTriangular" | custom-call | tf_op jit(solution)/shard_map/triangular_solve | solution.py:32
  394.7 17.5 %fusion.16 = bf16[1,256,3328]{1,2,0:T(8,128)(2,1)S(1)} fusion(f32[256,768]{0,1:T(8,128)S(1)} %fusion.30, f32[3328,768]{0,1:T(8,128)S(1)} %convolution_dynamic-update-slice_fusion, f32[256,4096]{0,1:T(8,128)S(1)} %bitcast.106), kind=kOutput, calls=%fused_computation.33 | convolution fusion | flops 7853441024 | bytes 16121856 | tf_op jit(solution)/shard_map/dot_general | solution.py:37
  413.9 18.8 %collective-permute-done = bf16[1,256,3328]{1,2,0:T(8,128)(2,1)S(1)} collective-permute-done((bf16[1,256,3328]{1,2,0:T(8,128)(2,1)S(1)}, bf16[1,256,3328]{1,2,0:T(8,128)(2,1)S(1)}, u32[]{:S(2)}, u32[]{:S(2)}) %collective-permute-start) | collective-permute-done | bytes 1703968 | tf_op jit(solution)/shard_map/ppermute | solution.py:14
  437.6 18.8 %collective-permute-done.1 = bf16[1,256,3328]{1,2,0:T(8,128)(2,1)S(1)} collective-permute-done((bf16[1,256,3328]{1,2,0:T(8,128)(2,1)S(1)}, bf16[1,256,3328]{1,2,0:T(8,128)(2,1)S(1)}, u32[]{:S(2)}, u32[]{:S(2)}) %collective-permute-start.1) | collective-permute-done | bytes 1703968 | tf_op jit(solution)/shard_map/ppermute | solution.py:14
  461.3 18.8 %collective-permute-done.2 = bf16[1,256,3328]{1,2,0:T(8,128)(2,1)S(1)} collective-permute-done((bf16[1,256,3328]{1,2,0:T(8,128)(2,1)S(1)}, bf16[1,256,3328]{1,2,0:T(8,128)(2,1)S(1)}, u32[]{:S(2)}, u32[]{:S(2)}) %collective-permute-start.2) | collective-permute-done | bytes 1703968 | tf_op jit(solution)/shard_map/ppermute | solution.py:14
  484.9 18.8 %collective-permute-done.3 = bf16[1,256,3328]{1,2,0:T(8,128)(2,1)S(1)} collective-permute-done((bf16[1,256,3328]{1,2,0:T(8,128)(2,1)S(1)}, bf16[1,256,3328]{1,2,0:T(8,128)(2,1)S(1)}, u32[]{:S(2)}, u32[]{:S(2)}) %collective-permute-start.3) | collective-permute-done | bytes 1703968 | tf_op jit(solution)/shard_map/ppermute | solution.py:14
  508.6 18.8 %collective-permute-done.4 = bf16[1,256,3328]{1,2,0:T(8,128)(2,1)S(1)} collective-permute-done((bf16[1,256,3328]{1,2,0:T(8,128)(2,1)S(1)}, bf16[1,256,3328]{1,2,0:T(8,128)(2,1)S(1)}, u32[]{:S(2)}, u32[]{:S(2)}) %collective-permute-start.4) | collective-permute-done | bytes 1703968 | tf_op jit(solution)/shard_map/ppermute | solution.py:14
  532.3 18.8 %collective-permute-done.5 = bf16[1,256,3328]{1,2,0:T(8,128)(2,1)} collective-permute-done((bf16[1,256,3328]{1,2,0:T(8,128)(2,1)S(1)}, bf16[1,256,3328]{1,2,0:T(8,128)(2,1)}, u32[]{:S(2)}, u32[]{:S(2)}) %collective-permute-start.5) | collective-permute-done | bytes 1703968 | tf_op jit(solution)/shard_map/ppermute | solution.py:14
  554.8 11.9 %copy.15 = bf16[1,2,256,8192]{2,3,1,0:T(8,128)(2,1)} copy(bf16[1,2,256,8192]{3,2,1,0:T(8,128)(2,1)} %param.11) | data formatting | bytes 16777216 | tf_op args[3]
  599.5 55.9 %while.20 = (s32[]{:T(128)}, f32[2,256,2,13,256]{1,4,3,2,0:T(8,128)}, s32[8]{0:T(128)S(1)}, s32[]{:T(128)}, pred[]{:T(512)}, /*index=5*/s32[8,13]{1,0:T(8,128)},...) while((s32[]{:T(128)}, f32[2,256,2,13,256]{1,4,3,2,0:T(8,128)}, ...), condition=%wide.region_15.16_spmd, body=%wide.region_12.15_spmd.sunk | while | flops 5963816 | bytes 32375320 | solution.py:66
  602.0 11.9 %conditional.2 = (f32[2,256,2,13,256]{1,4,3,2,0:T(8,128)}) conditional(s32[]{:T(128)} %convert_element_type.52, f32[2,256,2,13,256]{1,4,3,2,0:T(8,128)} %get-tuple-element.603, (s32[]{:T(128)}, s32[]{:T(128)}, f32[2,256,2,13,256]{1,4,3,2,0:T(8,128)}, s32[8,13]{1,0:T(8,128)}, s32[]{:T(128)}, /*index=5*/bf16[8,256,3328]{1,2,0:T(8,128)(2,1)}, ...), branch_computations={%region_13.13_spmd, %region_14.14_spmd} | conditional | flops 5963810 | bytes 32375100 | solution.py:64
  624.0 12.0 %conditional.2 = (f32[2,256,2,13,256]{1,4,3,2,0:T(8,128)}) conditional(s32[]{:T(128)} %convert_element_type.52, f32[2,256,2,13,256]{1,4,3,2,0:T(8,128)} %get-tuple-element.603, (s32[]{:T(128)}, s32[]{:T(128)}, f32[2,256,2,13,256]{1,4,3,2,0:T(8,128)}, s32[8,13]{1,0:T(8,128)}, s32[]{:T(128)}, /*index=5*/bf16[8,256,3328]{1,2,0:T(8,128)(2,1)}, ...), branch_computations={%region_13.13_spmd, %region_14.14_spmd} | conditional | flops 5963810 | bytes 32375100 | solution.py:64
  638.5 11.9 %conditional.2 = (f32[2,256,2,13,256]{1,4,3,2,0:T(8,128)}) conditional(s32[]{:T(128)} %convert_element_type.52, f32[2,256,2,13,256]{1,4,3,2,0:T(8,128)} %get-tuple-element.603, (s32[]{:T(128)}, s32[]{:T(128)}, f32[2,256,2,13,256]{1,4,3,2,0:T(8,128)}, s32[8,13]{1,0:T(8,128)}, s32[]{:T(128)}, /*index=5*/bf16[8,256,3328]{1,2,0:T(8,128)(2,1)}, ...), branch_computations={%region_13.13_spmd, %region_14.14_spmd} | conditional | flops 5963810 | bytes 32375100 | solution.py:64
  671.2 12.0 %copy.19 = bf16[1,2,256,8192]{3,2,1,0:T(8,128)(2,1)} copy(bf16[1,2,256,8192]{2,3,1,0:T(8,128)(2,1)} %bitcast.101) | data formatting | bytes 16777216 | tf_op jit(solution)/shard_map/broadcast_in_dim;reshape | solution.py:69
  (181 shorter events, 254.9 us)
Async XLA Ops:
  7.2 108.8 %all-gather.2.cloned.1.call-start = ((), (), s32[]{:S(2)}) async-start(), calls=%async_computation | async-start | bytes 13369344 | tf_op jit(solution)/shard_map/all_gather | solution.py:30
  115.9 1.7 slice-start.3
  340.6 8.6 %copy-start.17 = (f32[6,128,128]{1,2,0:T(8,128)}, f32[6,128,128]{1,2,0:T(8,128)S(1)}, u32[]{:S(2)}) copy-start(f32[6,128,128]{1,2,0:T(8,128)S(1)} %custom-call.51) | copy-start | bytes 1179652
  345.9 14.6 %slice-start = ((s8[12582912]{0:T(1024)(128)(4,1)}), s8[4194304]{0:T(1024)(128)(4,1)S(1)}, s32[]{:S(2)}) async-start(s8[12582912]{0:T(1024)(128)(4,1)} %bitcast.107), calls=%async_computation.1 | async-start | bytes 8388608
  349.2 11.3 %slice-start.1 = ((s8[12582912]{0:T(1024)(128)(4,1)}), s8[4194304]{0:T(1024)(128)(4,1)S(1)}, s32[]{:S(2)}) async-start(s8[12582912]{0:T(1024)(128)(4,1)} %bitcast.107), calls=%async_computation.2 | async-start | bytes 8388608
  351.0 9.6 %slice-start.2 = ((s8[12582912]{0:T(1024)(128)(4,1)}), s8[4194304]{0:T(1024)(128)(4,1)S(1)}, s32[]{:S(2)}) async-start(s8[12582912]{0:T(1024)(128)(4,1)} %bitcast.107), calls=%async_computation.3 | async-start | bytes 8388608
  357.3 3.2 copy-start.1
  360.6 5.2 copy-start.14
  392.5 2.2 copy-start
  394.7 17.5 %copy-start.2 = (f32[256,768]{0,1:T(8,128)}, f32[256,768]{0,1:T(8,128)S(1)}, u32[]{:S(2)}) copy-start(f32[256,768]{0,1:T(8,128)S(1)} %fusion.30) | copy-start | bytes 2359300
  412.2 20.5 %collective-permute-start = (bf16[1,256,3328]{1,2,0:T(8,128)(2,1)S(1)}, bf16[1,256,3328]{1,2,0:T(8,128)(2,1)S(1)}, u32[]{:S(2)}, u32[]{:S(2)}) collective-permute-start(bf16[1,256,3328]{1,2,0:T(8,128)(2,1)S(1)} %fusion.16), channel_id=1, source_target_pairs={{0,16},{16,32},{32,48},{48,64},{64,80},{80,96},{96,112},{112,0},{1... | collective-permute-start | bytes 5111816 | tf_op jit(solution)/shard_map/ppermute | solution.py:14
  433.9 22.5 %collective-permute-start.1 = (bf16[1,256,3328]{1,2,0:T(8,128)(2,1)S(1)}, bf16[1,256,3328]{1,2,0:T(8,128)(2,1)S(1)}, u32[]{:S(2)}, u32[]{:S(2)}) collective-permute-start(bf16[1,256,3328]{1,2,0:T(8,128)(2,1)S(1)} %collective-permute-done), channel_id=1, source_target_pairs={{0,16},{16,32},{32,48},{48,64},{64,80},{80,96},{96,112},{112,0},{1... | collective-permute-start | bytes 5111816 | tf_op jit(solution)/shard_map/ppermute | solution.py:14
  457.6 22.5 %collective-permute-start.2 = (bf16[1,256,3328]{1,2,0:T(8,128)(2,1)S(1)}, bf16[1,256,3328]{1,2,0:T(8,128)(2,1)S(1)}, u32[]{:S(2)}, u32[]{:S(2)}) collective-permute-start(bf16[1,256,3328]{1,2,0:T(8,128)(2,1)S(1)} %collective-permute-done.1), channel_id=1, source_target_pairs={{0,16},{16,32},{32,48},{48,64},{64,80},{80,96},{96,112},{112,0},{1... | collective-permute-start | bytes 5111816 | tf_op jit(solution)/shard_map/ppermute | solution.py:14
  481.3 22.5 %collective-permute-start.3 = (bf16[1,256,3328]{1,2,0:T(8,128)(2,1)S(1)}, bf16[1,256,3328]{1,2,0:T(8,128)(2,1)S(1)}, u32[]{:S(2)}, u32[]{:S(2)}) collective-permute-start(bf16[1,256,3328]{1,2,0:T(8,128)(2,1)S(1)} %collective-permute-done.2), channel_id=1, source_target_pairs={{0,16},{16,32},{32,48},{48,64},{64,80},{80,96},{96,112},{112,0},{1... | collective-permute-start | bytes 5111816 | tf_op jit(solution)/shard_map/ppermute | solution.py:14
  504.9 22.5 %collective-permute-start.4 = (bf16[1,256,3328]{1,2,0:T(8,128)(2,1)S(1)}, bf16[1,256,3328]{1,2,0:T(8,128)(2,1)S(1)}, u32[]{:S(2)}, u32[]{:S(2)}) collective-permute-start(bf16[1,256,3328]{1,2,0:T(8,128)(2,1)S(1)} %collective-permute-done.3), channel_id=1, source_target_pairs={{0,16},{16,32},{32,48},{48,64},{64,80},{80,96},{96,112},{112,0},{1... | collective-permute-start | bytes 5111816 | tf_op jit(solution)/shard_map/ppermute | solution.py:14
  528.6 22.5 %collective-permute-start.5 = (bf16[1,256,3328]{1,2,0:T(8,128)(2,1)S(1)}, bf16[1,256,3328]{1,2,0:T(8,128)(2,1)}, u32[]{:S(2)}, u32[]{:S(2)}) collective-permute-start(bf16[1,256,3328]{1,2,0:T(8,128)(2,1)S(1)} %collective-permute-done.4), channel_id=1, source_target_pairs={{0,16},{16,32},{32,48},{48,64},{64,80},{80,96},{96,112},{112,0},{1... | collective-permute-start | bytes 5111816 | tf_op jit(solution)/shard_map/ppermute | solution.py:14
  551.0 29.3 %collective-permute-start.6 = (bf16[1,256,3328]{1,2,0:T(8,128)(2,1)}, bf16[1,256,3328]{1,2,0:T(8,128)(2,1)}, u32[]{:S(2)}, u32[]{:S(2)}) collective-permute-start(bf16[1,256,3328]{1,2,0:T(8,128)(2,1)} %collective-permute-done.5), channel_id=1, source_target_pairs={{0,16},{16,32},{32,48},{48,64},{64,80},{80,96},{96,112},{112,0},{1... | collective-permute-start | bytes 5111816 | tf_op jit(solution)/shard_map/ppermute | solution.py:14
  569.4 9.8 %copy-start.3 = (f32[256,768]{0,1:T(8,128)S(1)}, f32[256,768]{0,1:T(8,128)}, u32[]{:S(2)}) copy-start(f32[256,768]{0,1:T(8,128)} %copy-done.2) | copy-start | bytes 2359300
  581.9 2.0 copy-start.13
  583.9 1.5 copy-start.11
  585.3 1.5 copy-start.9
  586.8 1.5 copy-start.7
  593.8 5.8 copy-start.18
  655.4 8.8 %copy-start.15 = (bf16[2,256,2,3,256]{1,4,3,2,0:T(8,128)(2,1)S(1)}, bf16[2,256,2,3,256]{1,4,3,2,0:T(8,128)(2,1)}, u32[]{:S(2)}) copy-start(bf16[2,256,2,3,256]{1,4,3,2,0:T(8,128)(2,1)} %slice.203) | copy-start | bytes 4718596
  (7 other events, 8.9 us)
Sparse Core Ops, SparseCore 0:
  15.0 100.8 all-gather.1
